TPU v7x, 512 devices: a whole 4x4x16 slice. The times are simulated.
512 devices in a mesh: row: 8 (over x_lo, y), col: 64 (over x_hi, z, core).
Axes of the slice: x: 4 (x_hi: 2, x_lo: 2; x = x_hi * 2 + x_lo), y: 4, z: 16, core: 2. Of those that a mesh axis runs over, the one named last changes fastest.
Arguments:
- right_side: float32 [8192, 16384], P('row', 'col'), may hold values from -8 to 8
- factor_panels: float32 [4, 256, 8192], P(None, 'col', 'row'), may hold values from -0.1875 to 0.1875
- inverses: float32 [4, 256, 256], P(None, 'col'), may hold values from -0.5 to 1.6, as said below
Outputs:
- solved: float32 [8192, 16384], P('row', 'col')
Inputs may be any that keep to these rules, and one draw needn't show every extreme that they name: inverses[k] is lower triangular with a diagonal between 0.6 and 1.6 and independent entries below it.
All inputs are finite; a program needn't handle non-finite values.
Results may differ from a plain program's by a relative error of at most 0.0001.
Values sent between devices are 32-bit elements; how exact they have to be, the bound alone decides.
A program may use at most 64 MiB of HBM per device.

v0:
```python
import jax
import jax.numpy as jnp
from jax import lax
from jax.sharding import PartitionSpec as P


def spread(value, axis, root):
    mine = lax.axis_index(axis) == root
    return lax.psum(jnp.where(mine, value, jnp.zeros_like(value)), axis)


def contract(factor_rows, answer):
    return lax.dot_general(
        factor_rows,
        answer,
        (((0,), (0,)), ((), ())),
        precision=lax.Precision.HIGHEST,
        preferred_element_type=jnp.float32,
    )


def solve_block(work, inverses, panel, group_count, block_size):
    local = panel // group_count
    current = work[local * block_size : (local + 1) * block_size]
    inverse = lax.all_gather(inverses[panel], "col", axis=0, tiled=True)
    answer = jnp.dot(
        inverse, current, precision=lax.Precision.HIGHEST, preferred_element_type=jnp.float32
    )
    return spread(answer, "row", panel % group_count)


def place(work, answer, panel, group_count, group_index, block_size):
    local = panel // group_count
    current = work[local * block_size : (local + 1) * block_size]
    chosen = jnp.where(group_index == panel % group_count, answer, current)
    return work.at[local * block_size : (local + 1) * block_size].set(chosen)


def per_device(right_side, factor_panels, inverses):
    group_count = lax.axis_size("row")
    group_index = lax.axis_index("row")
    local_rows = right_side.shape[0]
    block_size = inverses.shape[2]
    panels = inverses.shape[0]
    local_block = jnp.arange(local_rows, dtype=jnp.int32) // block_size
    rank = local_block * group_count + group_index
    work = right_side
    for panel in range(panels):
        answer = solve_block(work, inverses, panel, group_count, block_size)
        work = place(work, answer, panel, group_count, group_index, block_size)
        update = contract(lax.all_gather(factor_panels[panel], "col", axis=0, tiled=True), answer)
        work = work - jnp.where((rank > panel)[:, None], update, jnp.zeros_like(update))
    return work


def solution(mesh):
    in_specs = (P("row", "col"), P(None, "col", "row"), P(None, "col", None))
    out_specs = P("row", "col")
    return jax.shard_map(
        per_device, mesh=mesh, in_specs=in_specs, out_specs=out_specs, check_vma=False
    )
```

profile of v0, /device:TPU:1, one launch (start us, length us, event | category | flops | bytes accessed | tf_op | source)
XLA Modules:
  0.0 670.4 jit_solution(9564360170566659969)
XLA Ops:
  7.4 0.0 copy-start
  7.4 0.0 all-reduce.5.cloned.1.call-start
  7.4 0.8 fusion.41
  8.2 85.3 %all-gather = f32[1,256,256]{2,0,1:T(1,128)S(1)} all-gather(f32[1,4,256]{2,0,1:T(1,128)S(1)} %copy.32), channel_id=2, replica_groups=mesh['row'=8,'col'=64] {'col'}, dimensions={1}, use_global_device_ids=true | all-gather | bytes 266240 | tf_op jit(solution)/shard_map/all_gather | solution.py:25
  93.5 2.0 convolution_select_fusion.7
  95.5 0.0 copy-start.5
  95.5 0.0 all-reduce.5.cloned.1.call-update
  95.5 0.0 all-gather.13.cloned.1.call-start
  95.6 0.8 copy-done.5
  96.3 0.6 copy.33
  97.0 0.0 all-gather.13.cloned.1.call-update
  97.0 0.0 all-reduce.7.cloned.1.call-start
  97.0 0.0 copy-done
  97.0 0.3 copy.11
  97.4 72.3 %all-gather.2 = f32[1,256,256]{2,0,1:T(1,128)S(1)} all-gather(f32[1,4,256]{2,0,1:T(1,128)S(1)} %copy.34), channel_id=4, replica_groups=mesh['row'=8,'col'=64] {'col'}, dimensions={1}, use_global_device_ids=true | all-gather | bytes 266240 | tf_op jit(solution)/shard_map/all_gather | solution.py:25
  169.7 0.0 all-reduce.5.cloned.1.call-done
  169.7 1.0 slice_select_fusion
  170.7 0.1 copy.12
  170.8 0.0 copy-start.1
  170.9 58.4 %all-gather.13.cloned.1.call-done = f32[1,256,1024]{2,0,1:T(1,128)} async-done(((f32[1,4,1024]{2,0,1:T(1,128)}), f32[1,256,1024]{2,0,1:T(1,128)}) %all-gather.13.cloned.1.call-update) | async-done | bytes 1048592 | tf_op jit(solution)/shard_map/all_gather | solution.py:51
  229.3 0.0 copy-done.1
  229.3 2.4 fusion.4
  231.7 1.1 fusion.10
  232.8 0.0 all-reduce.7.cloned.1.call-update
  232.8 0.0 all-gather.15.cloned.1.call-start
  232.9 0.6 copy.35
  233.5 0.0 all-gather.15.cloned.1.call-update
  233.5 0.0 all-reduce.9.cloned.1.call-start
  233.6 75.3 %all-gather.4 = f32[1,256,256]{2,0,1:T(1,128)S(1)} all-gather(f32[1,4,256]{2,0,1:T(1,128)S(1)} %copy.36), channel_id=6, replica_groups=mesh['row'=8,'col'=64] {'col'}, dimensions={1}, use_global_device_ids=true | all-gather | bytes 266240 | tf_op jit(solution)/shard_map/all_gather | solution.py:25
  308.9 3.6 all-reduce.7.cloned.1.call-done
  312.5 0.0 copy-start.3
  312.5 0.1 select_dynamic-update-slice_fusion.2
  312.6 59.7 %all-gather.15.cloned.1.call-done = f32[1,256,1024]{2,0,1:T(1,128)} async-done(((f32[1,4,1024]{2,0,1:T(1,128)}), f32[1,256,1024]{2,0,1:T(1,128)}) %all-gather.15.cloned.1.call-update) | async-done | bytes 1048592 | tf_op jit(solution)/shard_map/all_gather | solution.py:51
  372.3 0.0 copy-done.3
  372.3 2.4 fusion.5
  374.7 1.1 fusion.9
  375.9 0.0 all-reduce.9.cloned.1.call-update
  375.9 0.0 all-gather.17.cloned.1.call-start
  375.9 0.6 copy.37
  376.6 0.0 all-gather.17.cloned.1.call-update
  376.6 0.0 all-reduce.11.cloned.1.call-start
  376.7 75.3 %all-gather.6 = f32[1,256,256]{2,0,1:T(1,128)S(1)} all-gather(f32[1,4,256]{2,0,1:T(1,128)S(1)} %copy.38), channel_id=8, replica_groups=mesh['row'=8,'col'=64] {'col'}, dimensions={1}, use_global_device_ids=true | all-gather | bytes 266240 | tf_op jit(solution)/shard_map/all_gather | solution.py:25
  452.0 3.6 all-reduce.9.cloned.1.call-done
  455.6 0.0 copy-start.2
  455.6 0.1 select_dynamic-update-slice_fusion.1
  455.7 60.2 %all-gather.17.cloned.1.call-done = f32[1,256,1024]{2,0,1:T(1,128)} async-done(((f32[1,4,1024]{2,0,1:T(1,128)}), f32[1,256,1024]{2,0,1:T(1,128)}) %all-gather.17.cloned.1.call-update) | async-done | bytes 1048592 | tf_op jit(solution)/shard_map/all_gather | solution.py:51
  515.9 0.0 copy-done.2
  515.9 2.4 fusion.6
  518.3 1.1 fusion.8
  519.4 0.0 all-reduce.11.cloned.1.call-update
  519.5 0.0 all-gather.19.cloned.1.call-start
  519.5 0.6 copy.39
  520.1 0.1 all-gather.19.cloned.1.call-update
  520.2 79.0 %all-reduce.11.cloned.1.call-done = f32[256,256]{0,1:T(8,128)} async-done(((f32[256,256]{0,1:T(8,128)}), f32[256,256]{0,1:T(8,128)}) %all-reduce.11.cloned.1.call-update) | async-done | bytes 262160 | tf_op jit(solution)/shard_map/psum | solution.py:9
  599.2 0.0 copy-start.4
  599.2 0.1 select_dynamic-update-slice_fusion
  599.3 60.0 %all-gather.19.cloned.1.call-done = f32[1,256,1024]{2,0,1:T(1,128)} async-done(((f32[1,4,1024]{2,0,1:T(1,128)}), f32[1,256,1024]{2,0,1:T(1,128)}) %all-gather.19.cloned.1.call-update) | async-done | bytes 1048592 | tf_op jit(solution)/shard_map/all_gather | solution.py:51
  659.3 0.0 copy-done.4
  659.3 2.4 fusion.7
  661.7 1.3 copy.23
  (10 shorter events, 0.1 us)
Async XLA Ops:
  7.4 89.7 %copy-start = (f32[1024,256]{1,0:T(8,128)S(1)}, f32[1024,256]{1,0:T(8,128)}, u32[]{:S(2)}) copy-start(f32[1024,256]{1,0:T(8,128)} %param.11) | copy-start | bytes 3145732
  7.4 162.4 %all-reduce.5.cloned.1.call-start = ((), (), s32[]{:S(2)}) async-start(), calls=%async_computation | async-start | bytes 524288 | tf_op jit(solution)/shard_map/psum | solution.py:9
  95.5 0.8 copy-start.5
  95.5 133.7 %all-gather.13.cloned.1.call-start = ((), (), s32[]{:S(2)}) async-start(), calls=%async_computation.4 | async-start | bytes 1064960 | tf_op jit(solution)/shard_map/all_gather | solution.py:51
  97.0 215.5 %all-reduce.7.cloned.1.call-start = ((), (), s32[]{:S(2)}) async-start(), calls=%async_computation.1 | async-start | bytes 524288 | tf_op jit(solution)/shard_map/psum | solution.py:9
  170.8 58.4 %copy-start.1 = (f32[256,256]{1,0:T(8,128)S(1)}, f32[256,256]{1,0:T(8,128)}, u32[]{:S(2)}) copy-start(f32[256,256]{1,0:T(8,128)} %all-reduce.5.cloned.1.call-done) | copy-start | bytes 786436
  232.8 139.5 %all-gather.15.cloned.1.call-start = ((), (), s32[]{:S(2)}) async-start(), calls=%async_computation.5 | async-start | bytes 1064960 | tf_op jit(solution)/shard_map/all_gather | solution.py:51
  233.5 222.1 %all-reduce.9.cloned.1.call-start = ((), (), s32[]{:S(2)}) async-start(), calls=%async_computation.2 | async-start | bytes 524288 | tf_op jit(solution)/shard_map/psum | solution.py:9
  312.5 59.8 %copy-start.3 = (f32[256,256]{0,1:T(8,128)S(1)}, f32[256,256]{0,1:T(8,128)}, u32[]{:S(2)}) copy-start(f32[256,256]{0,1:T(8,128)} %all-reduce.7.cloned.1.call-done) | copy-start | bytes 786436
  375.9 140.0 %all-gather.17.cloned.1.call-start = ((), (), s32[]{:S(2)}) async-start(), calls=%async_computation.6 | async-start | bytes 1064960 | tf_op jit(solution)/shard_map/all_gather | solution.py:51
  376.6 222.6 %all-reduce.11.cloned.1.call-start = ((), (), s32[]{:S(2)}) async-start(), calls=%async_computation.3 | async-start | bytes 524288 | tf_op jit(solution)/shard_map/psum | solution.py:9
  455.6 60.3 %copy-start.2 = (f32[256,256]{0,1:T(8,128)S(1)}, f32[256,256]{0,1:T(8,128)}, u32[]{:S(2)}) copy-start(f32[256,256]{0,1:T(8,128)} %all-reduce.9.cloned.1.call-done) | copy-start | bytes 786436
  519.5 139.8 %all-gather.19.cloned.1.call-start = ((), (), s32[]{:S(2)}) async-start(), calls=%async_computation.7 | async-start | bytes 1064960 | tf_op jit(solution)/shard_map/all_gather | solution.py:51
  599.2 60.1 %copy-start.4 = (f32[256,256]{0,1:T(8,128)S(1)}, f32[256,256]{0,1:T(8,128)}, u32[]{:S(2)}) copy-start(f32[256,256]{0,1:T(8,128)} %all-reduce.11.cloned.1.call-done) | copy-start | bytes 786436
Sparse Core Ops, SparseCore 0:
  95.6 73.3 all-reduce.4
  232.9 79.5 all-reduce.6
  376.0 79.5 all-reduce.8
  519.6 79.5 all-reduce.10
Sparse Core Ops, SparseCore 1:
  99.8 129.4 all-gather.12
  236.6 135.7 all-gather.14
  380.2 135.7 all-gather.16
  523.5 135.7 all-gather.18
where the time goes:
time: 671 us; the launch traced here: 670 us
  waiting for transfers between devices  325 us (48%)
  blocking collectives  308 us (46%)
  between operations  15 us (2%)
  matrix products  14.9 us (2%)
    all_gather x4, blocking collectives, solve_block(): inverse = lax.all_gather(inverses[panel], 'col', axis=0, tiled=True)  308 us
    all_gather x4, waiting for transfers between devices, per_device(): lax.all_gather(factor_panels[panel], 'col', axis=0, tiled=True)  238 us
    psum x4, waiting for transfers between devices, spread(): return lax.psum(jnp.where(mine, value, jnp.zeros_like(value)), axis)  86.2 us
  transfers between devices with their start and end apart: 8, of which 7 were waited for; matrix products, arithmetic and copies ran while one was open for 1% of the time, Pallas kernels for 0%

commit v1 on v0

v1 whole, which is shorter than its diff:
```python
import jax
import jax.numpy as jnp
from jax import lax
from jax.experimental import pallas as pl
from jax.experimental.pallas import tpu as pltpu
from jax.sharding import PartitionSpec as P

MESH = pl.DeviceIdType.MESH
NZ = 16
PANELS = 4
OWNERS = 4
NB = 256
PAIRS = 6
BF16 = jnp.bfloat16
F32 = jnp.float32


def pair(m, k):
    return k * (k - 1) // 2 + m


def split(value):
    high = value.astype(BF16)
    low = (value - high.astype(F32)).astype(BF16)
    return high, low


def dot3(a, b, dims):
    def one(p, q):
        return lax.dot_general(p, q, (dims, ((), ())), preferred_element_type=F32)

    return one(a[0], b[0]) + (one(a[0], b[1]) + one(a[1], b[0]))


def kernel(
    rs_hbm, fac, inv, out_hbm,
    big, small, bvec, rs, xhi, xlo,
    ring_s, ring_r, x_s, x_r, sib_s, sibx_s, sib_ra, sib_rb,
    ch_s, ch_r, b_s, b_r, loc_s, out_s,
):
    row = lax.axis_index("row")
    col = lax.axis_index("col")
    xl, y = row // 4, row % 4
    xh, z, q = col // 32, (col // 2) % NZ, col % 2

    def at(row_to, xh_to, z_to, q_to):
        return (row_to, (xh_to * NZ + z_to) * 2 + q_to)

    up, down = at(row, xh, (z + 1) % NZ, q), at(row, xh, (z + NZ - 1) % NZ, q)
    towards = (up, down)
    sibling = at(row, xh, z, 1 - q)
    peer = at(row, 1 - xh, z, q)
    others = [at((row + i % 8) % 8, (xh + i // 8) % 2, z, q) for i in range(1, 16)]

    load_rs = pltpu.make_async_copy(rs_hbm, rs, loc_s.at[0])
    load_rs.start()
    own_big = pltpu.make_async_copy(fac, big.at[q, xh, z], loc_s.at[1])
    own_big.start()
    own_inv = pltpu.make_async_copy(inv, small.at[q, z, xh, pl.ds(0, PANELS)], loc_s.at[2])
    own_inv.start()

    barrier = pltpu.get_barrier_semaphore()
    greet = [up, down, sibling] + others
    for device in greet:
        pl.semaphore_signal(barrier, inc=1, device_id=device, device_id_type=MESH)
    pl.semaphore_wait(barrier, len(greet))

    def remote(src, dst, send, recv, device):
        return pltpu.make_async_remote_copy(
            src_ref=src, dst_ref=dst, send_sem=send, recv_sem=recv,
            device_id=device, device_id_type=MESH,
        )

    def chunk(origin, c):
        if c < 2:
            return small.at[q, origin, c]
        return big.at[q, xh, origin, pl.ds(2 * (c - 2), 2)]

    def ring(step, d, c):
        origin = (z + NZ - (step - 1)) % NZ if d == 0 else (z + step - 1) % NZ
        ref = chunk(origin, c)
        return remote(ref, ref, ring_s.at[d, step - 1, c], ring_r.at[d, step - 1, c], towards[d])

    def arrival(step, d, c):
        origin = (z + NZ - step) % NZ if d == 0 else (z + step) % NZ
        ref = chunk(origin, c)
        return origin, remote(
            ref, ref, ring_s.at[d, step - 1, c], ring_r.at[d, step - 1, c], towards[d]
        )

    def to_sibling(origin, slot, d, c):
        ref = chunk(origin, c)
        recv = sib_ra if c < 2 else sib_rb
        return remote(ref, ref, sib_s.at[d, slot, c], recv.at[0], sibling)

    def to_peer(origin, slot, d, c):
        ref = chunk(origin, c)
        return remote(ref, ref, x_s.at[d, slot, c - 2], x_r.at[d, slot], peer)

    def from_peer(origin, slot, d):
        ref = big.at[q, 1 - xh, origin]
        return remote(ref, ref, sibx_s.at[d, slot], x_r.at[d, slot], peer)

    def from_peer_half(origin, slot, d, c):
        ref = big.at[q, 1 - xh, origin, pl.ds(2 * (c - 2), 2)]
        return remote(ref, ref, sibx_s.at[d, slot], x_r.at[d, slot], peer)

    def peer_to_sibling(origin, slot, d):
        ref = big.at[q, 1 - xh, origin]
        return remote(ref, ref, sibx_s.at[d, slot], sib_rb.at[0], sibling)

    for k in (1, 2, 3):

        @pl.when(row == k)
        def _(k=k):
            place = pl.ds(PANELS + pair(0, k), k)
            src = fac.at[pl.ds(0, k), :, pl.ds(0, NB)]
            dst = small.at[q, z, xh, place]
            for i, device in enumerate(others):
                remote(src, dst, ch_s.at[i], ch_r.at[k - 1, xh], device).start()
            pltpu.make_async_copy(src, dst, ch_r.at[k - 1, xh]).start()

    inv_out = remote(
        inv, small.at[q, z, xh, pl.ds(0, PANELS)], ch_s.at[15], ch_r.at[3, 0], peer
    )
    inv_out.start()

    own_big.wait()
    for c in (2, 3):
        for d in (0, 1):
            ring(1, d, c).start()
        to_peer(z, 0, 0, c).start()
        to_sibling(z, 0, 0, c).start()

    head = pl.ds(0, NB)
    for k in range(OWNERS):

        @pl.when(row == k)
        def _(k=k):
            for i, device in enumerate(
                [at((k + 1) % 4, xh, z, q), at((k + 3) % 4, xh, z, q), at((k + 2) % 4, xh, z, q), at(k + 4, xh, z, q)]
            ):
                remote(rs_hbm.at[head], bvec.at[k], b_s.at[i], b_r.at[k], device).start()
            pltpu.make_async_copy(rs_hbm.at[head], bvec.at[k], b_r.at[k]).start()

    own_inv.wait()
    inv_in = small.at[q, z, 1 - xh, pl.ds(0, PANELS)]
    remote(inv, inv_in, ch_s.at[15], ch_r.at[3, 0], peer).wait_recv()
    for k in (1, 2, 3):
        for half in (0, 1):
            ref = small.at[q, z, half, pl.ds(PANELS + pair(0, k), k)]
            pltpu.make_async_copy(ref, ref, ch_r.at[k - 1, half]).wait()
    for c in (0, 1):
        for d in (0, 1):
            ring(1, d, c).start()
        to_sibling(z, 0, 0, c).start()

    def forward_b():
        for k in range(OWNERS):

            @pl.when(row == OWNERS + k)
            def _(k=k):
                pltpu.make_async_copy(rs_hbm.at[head], bvec.at[k], b_r.at[k]).wait()
                for i, device in enumerate(
                    [at(4 + (k + 1) % 4, xh, z, q), at(4 + (k + 3) % 4, xh, z, q), at(4 + (k + 2) % 4, xh, z, q)]
                ):
                    remote(bvec.at[k], bvec.at[k], b_s.at[i], b_r.at[k], device).start()

    def peer_arrivals(step):
        for d in (0, 1):
            origin = (z + NZ - step) % NZ if d == 0 else (z + step) % NZ
            from_peer(origin, step, d).wait_recv()
            peer_to_sibling(origin, step, d).start()

    def take(step, d, c, send):
        origin, copy = arrival(step, d, c)
        copy.wait_recv()
        if send:
            ring(step + 1, d, c).start()
        if c >= 2:
            to_peer(origin, step, d, c).start()
        to_sibling(origin, step, d, c).start()

    for c in (2, 3, 0, 1):
        for d in (0, 1):
            take(1, d, c, True)
    forward_b()
    from_peer(z, 0, 0).wait_recv()
    peer_to_sibling(z, 0, 0).start()

    def body(step, carry):
        for c in (0, 1, 2, 3):
            for d in (0, 1):
                take(step, d, c, True)
        peer_arrivals(step - 1)
        return carry

    lax.fori_loop(2, 7, body, 0)
    for c in (0, 1, 2, 3):
        for d in (0, 1):
            take(7, d, c, c % 2 == d)
    peer_arrivals(6)
    for c in (0, 1, 2, 3):
        take(8, c % 2, c, False)
    peer_arrivals(7)

    sib_small = small.at[1 - q]
    pltpu.make_async_copy(sib_small, sib_small, sib_ra.at[0]).wait()

    def square(index):
        halves = [
            jnp.concatenate([small[0, :, half, index], small[1, :, half, index]], axis=1).reshape(NB // 2, NB)
            for half in (0, 1)
        ]
        return jnp.concatenate(halves, axis=0)

    solved = []
    for k in range(PANELS):
        @pl.when(row != OWNERS + k)
        def _(k=k):
            pltpu.make_async_copy(rs_hbm.at[head], bvec.at[k], b_r.at[k]).wait()

        work = bvec[k]
        for m in range(k):
            work = work - dot3(split(square(PANELS + pair(m, k))), solved[m], ((0,), (0,)))
        answer = dot3(split(square(k)), split(work), ((1,), (0,)))

        if k == 0:
            load_rs.wait()

        @pl.when(row == k)
        def _(answer=answer):
            rs[head, :] = answer

        high, low = split(answer)
        solved.append((high, low))
        xhi[k] = high
        xlo[k] = low
        if k == 1:
            for c in (2, 3):
                origin = (z + NZ // 2) % NZ
                d = c % 2
                from_peer_half(origin, 8, d, c).wait_recv()
            peer_to_sibling((z + NZ // 2) % NZ, 8, 0).start()

    sib_big = big.at[1 - q]
    pltpu.make_async_copy(sib_big, sib_big, sib_rb.at[0]).wait()

    def update(block):
        lanes = pl.ds(pl.multiple_of(block * NB, NB), NB)
        total = jnp.zeros((NB, NB), F32)
        for k in range(PANELS):
            for half in (0, 1):
                factor = jnp.concatenate(
                    [big[0, half, :, k, :, lanes], big[1, half, :, k, :, lanes]], axis=1
                ).reshape(NB // 2, NB)
                rows_k = pl.ds(half * (NB // 2), NB // 2)
                x = (xhi[k, rows_k, :], xlo[k, rows_k, :])
                total = total + dot3(split(factor), x, ((0,), (0,)))
        rows = pl.ds(pl.multiple_of(block * NB, NB), NB)
        rs[rows, :] = rs[rows, :] - total

    def store(block):
        rows = pl.ds(pl.multiple_of(block * NB, NB), NB)
        return pltpu.make_async_copy(rs.at[rows], out_hbm.at[rows], out_s.at[block])

    @pl.when(row >= OWNERS)
    def _():
        update(0)

    store(0).start()

    def blocks(block, carry):
        update(block)
        store(block).start()
        return carry

    lax.fori_loop(1, 4, blocks, 0)

    for c in (2, 3):
        to_peer(z, 0, 0, c).wait_send()
    for c in range(4):
        to_sibling(z, 0, 0, c).wait_send()
    peer_to_sibling(z, 0, 0).wait_send()
    inv_out.wait_send()

    def drain(step, carry):
        for d in (0, 1):
            for c in range(4):
                ring(step, d, c).wait_send()
                to_sibling(z, step, d, c).wait_send()
                if c >= 2:
                    to_peer(z, step, d, c).wait_send()
            peer_to_sibling(z, step, d).wait_send()
        return carry

    lax.fori_loop(1, 8, drain, 0)
    for c in range(4):
        d = c % 2
        ring(8, d, c).wait_send()
        to_sibling(z, 8, d, c).wait_send()
        if c >= 2:
            to_peer(z, 8, d, c).wait_send()
    peer_to_sibling(z, 8, 0).wait_send()

    for k in (1, 2, 3):

        @pl.when(row == k)
        def _(k=k):
            src = fac.at[pl.ds(0, k), :, pl.ds(0, NB)]
            dst = small.at[q, z, xh, pl.ds(PANELS + pair(0, k), k)]
            for i, device in enumerate(others):
                remote(src, dst, ch_s.at[i], ch_r.at[k - 1, xh], device).wait_send()

    @pl.when(row < OWNERS)
    def _():
        for i in range(4):
            remote(rs_hbm.at[head], bvec.at[0], b_s.at[i], b_r.at[0], peer).wait_send()

    @pl.when(row >= OWNERS)
    def _():
        for i in range(3):
            remote(bvec.at[0], bvec.at[0], b_s.at[i], b_r.at[0], peer).wait_send()

    def finish(block, carry):
        store(block).wait()
        return carry

    lax.fori_loop(0, 4, finish, 0)


def per_device(right_side, factor_panels, inverses):
    rows, columns = right_side.shape
    dma = pltpu.SemaphoreType.DMA
    return pl.pallas_call(
        kernel,
        name="solve",
        out_shape=jax.ShapeDtypeStruct((rows, columns), F32),
        in_specs=[
            pl.BlockSpec(memory_space=pl.ANY),
            pl.BlockSpec(memory_space=pltpu.VMEM),
            pl.BlockSpec(memory_space=pltpu.VMEM),
        ],
        out_specs=pl.BlockSpec(memory_space=pl.ANY),
        scratch_shapes=[
            pltpu.VMEM((2, 2, NZ, PANELS, 4, rows), F32),
            pltpu.VMEM((2, NZ, 2, PANELS + PAIRS, 4, NB), F32),
            pltpu.VMEM((OWNERS, NB, columns), F32),
            pltpu.VMEM((rows, columns), F32),
            pltpu.VMEM((PANELS, NB, columns), BF16),
            pltpu.VMEM((PANELS, NB, columns), BF16),
            dma((2, 8, 4)),
            dma((2, 8, 4)),
            dma((2, 9, 2)),
            dma((2, 9)),
            dma((2, 9, 4)),
            dma((2, 9)),
            dma((1,)),
            dma((1,)),
            dma((16,)),
            dma((4, 2)),
            dma((4,)),
            dma((4,)),
            dma((3,)),
            dma((4,)),
        ],
        compiler_params=pltpu.CompilerParams(
            collective_id=0, has_side_effects=True, vmem_limit_bytes=48 << 20
        ),
        cost_estimate=pl.CostEstimate(flops=1 << 31, bytes_accessed=8 << 20, transcendentals=0),
    )(right_side, factor_panels, inverses)


def solution(mesh):
    in_specs = (P("row", "col"), P(None, "col", "row"), P(None, "col", None))
    return jax.shard_map(
        per_device, mesh=mesh, in_specs=in_specs, out_specs=P("row", "col"), check_vma=False
    )
```

time: 671 us -> 66.1 us (0.10)
  waiting for transfers between devices: 325 us -> 0 us
  blocking collectives: 308 us -> 0 us
  Pallas kernels: 0 us -> 62.1 us
  between operations: 15 us -> 0.01 us
  matrix products: 14.9 us -> 0 us
    all_gather x4 -> x0, blocking collectives: 308 us -> none  [solve_block(): inverse = lax.all_gather(inverses[panel], 'col', axis=0, tiled=True)]
    all_gather x4 -> x0, waiting for transfers between devices: 238 us -> none  [per_device(): lax.all_gather(factor_panels[panel], 'col', axis=0, tiled=True)]
    psum x4 -> x0, waiting for transfers between devices: 86.2 us -> none  [spread(): return lax.psum(jnp.where(mine, value, jnp.zeros_like(value)), axis)]
    pallas_call x0 -> x1, Pallas kernels: none -> 62.1 us  [per_device(): pl.pallas_call(kernel, name='solve', out_shape=jax.ShapeDtypeStruct((rows...]
    dot_general x8 -> x0, matrix products: 14.9 us -> none  [the longest x4 9.52 us: contract(): lax.dot_general(factor_rows, answer, (((0,), (0,)), ((), ())), precision=...]
  transfers between devices with their start and end apart: 8 -> 0, of which waited for: 7 -> 0; matrix products, arithmetic and copies ran while one was open for 1% -> 0% of each run, Pallas kernels for 0% -> 0%
where the time goes in v1:
time: 66.1 us; the launch traced here: 65.9 us
  Pallas kernels  62.1 us (94%)
  local copies, waits for them, and re-layouts  3.75 us (6%)
    pallas_call x1, Pallas kernels, per_device(): pl.pallas_call(kernel, name='solve', out_shape=jax.ShapeDtypeStruct((rows...  62.1 us
    unnamed x7, local copies, waits for them, and re-layouts  3.75 us

profile of v1, /device:TPU:1, one launch (start us, length us, event | category | flops | bytes accessed | tf_op | source)
XLA Modules:
  0.0 65.9 jit_solution(10102596533810659892)
XLA Ops:
  0.0 0.0 copy-start
  0.0 1.2 %copy-done = f32[1024,256]{1,0:T(8,128)S(1)} copy-done((f32[1024,256]{1,0:T(8,128)S(1)}, f32[1024,256]{1,0:T(8,128)}, u32[]{:S(2)}) %copy-start) | copy-done | bytes 1048600
  1.2 0.0 copy-start.1
  1.2 0.8 %copy-done.1 = f32[4,4,1024]{2,1,0:T(4,128)S(1)} copy-done((f32[4,4,1024]{2,1,0:T(4,128)S(1)}, f32[4,4,1024]{2,1,0:T(4,128)}, u32[]{:S(2)}) %copy-start.1) | copy-done | bytes 65560
  2.1 0.0 copy-start.2
  2.1 0.7 %copy-done.2 = f32[4,4,256]{2,1,0:T(4,128)S(1)} copy-done((f32[4,4,256]{2,1,0:T(4,128)S(1)}, f32[4,4,256]{2,1,0:T(4,128)}, u32[]{:S(2)}) %copy-start.2) | copy-done | bytes 16408
  2.8 62.1 %solve.1 = f32[1024,256]{1,0:T(8,128)S(1)} custom-call(f32[1024,256]{1,0:T(8,128)S(1)} %copy-done, f32[4,4,1024]{2,1,0:T(4,128)S(1)} %copy-done.1, f32[4,4,256]{2,1,0:T(4,128)S(1)} %copy-done.2), custom_call_target="tpu_custom_call" | custom-call | flops 2147483648 | bytes 8388608 | tf_op jit(solution)/shard_map/solve/pallas_call | solution.py:335
  64.9 1.0 %copy.5 = f32[1024,256]{1,0:T(8,128)} copy(f32[1024,256]{1,0:T(8,128)S(1)} %solve.1) | data formatting | bytes 2097152
Async XLA Ops:
  0.0 1.2 %copy-start = (f32[1024,256]{1,0:T(8,128)S(1)}, f32[1024,256]{1,0:T(8,128)}, u32[]{:S(2)}) copy-start(f32[1024,256]{1,0:T(8,128)} %rs_hbm.1) | copy-start | bytes 3145732
  1.2 0.8 %copy-start.1 = (f32[4,4,1024]{2,1,0:T(4,128)S(1)}, f32[4,4,1024]{2,1,0:T(4,128)}, u32[]{:S(2)}) copy-start(f32[4,4,1024]{2,1,0:T(4,128)} %fac.1) | copy-start | bytes 196612
  2.1 0.7 %copy-start.2 = (f32[4,4,256]{2,1,0:T(4,128)S(1)}, f32[4,4,256]{2,1,0:T(4,128)}, u32[]{:S(2)}) copy-start(f32[4,4,256]{2,1,0:T(4,128)} %inv.1) | copy-start | bytes 49156

commit v2 on v0

v2 whole, which is shorter than its diff:
```python
import jax
import jax.numpy as jnp
from jax import lax
from jax.experimental import pallas as pl
from jax.experimental.pallas import tpu as pltpu
from jax.sharding import PartitionSpec as P

MESH = pl.DeviceIdType.MESH
NZ = 16
PANELS = 4
OWNERS = 4
NB = 256
HALF = 128
CHUNKS = ((0, 2), (2, 2))
EXTRA = len(CHUNKS)
SLOTS = 5
BF16 = jnp.bfloat16
F32 = jnp.float32

INVERSE = {0: (0, 2), 1: (0, 3), 2: (0, 4), 3: (1, 4)}
BLOCK = {(0, 2): (0, 0), (1, 2): (0, 1), (0, 1): (1, 0), (0, 3): (1, 1), (1, 3): (1, 2), (2, 3): (1, 3)}


RING, RING_X, TREE, Y, X, PANEL, SIB, SIB_X, SIB_SMALL, SIB_PEER = range(10)


def split(value):
    high = value.astype(BF16)
    low = (value - high.astype(F32)).astype(BF16)
    return high, low


def dot3(a, b, dims):
    def one(p, q):
        return lax.dot_general(p, q, (dims, ((), ())), preferred_element_type=F32)

    return one(a[0], b[0]) + (one(a[0], b[1]) + one(a[1], b[0]))


def kernel(
    rs_hbm, fac, inv, out,
    big, small, bvec, xhi, xlo, ahi, alo,
    send, ring_r, tree_r, y_r, x_r, p_r, sib_r,
    ch_s, ch_r, b_s, b_r, loc_s,
):
    row = lax.axis_index("row")
    col = lax.axis_index("col")
    y, par = row % 4, row % 2
    xh, z, q = col // 32, (col // 2) % NZ, col % 2

    def at(row_to, xh_to, z_to, q_to):
        return (row_to, (xh_to * NZ + z_to) * 2 + q_to)

    def along_z(hop):
        return at(row, xh, (z + NZ + hop) % NZ, q)

    def along_y(hop):
        return at((row // 4) * 4 + (y + 4 + hop) % 4, xh, z, q)

    sibling = at(row, xh, z, 1 - q)
    peer = at(row, 1 - xh, z, q)
    others = [at((row + i % 8) % 8, (xh + i // 8) % 2, z, q) for i in range(1, 16)]
    alike = [at((row + 2 * (i % 4)) % 8, (xh + i // 4) % 2, z, q) for i in range(1, 8)]

    own_big = pltpu.make_async_copy(fac, big.at[q, xh, z], loc_s.at[1])
    own_big.start()
    load_rs = pltpu.make_async_copy(rs_hbm, out, loc_s.at[0])
    load_rs.start()

    barrier = pltpu.get_barrier_semaphore()
    greet = [along_z(hop) for hop in (1, -1, 2, -2)] + [sibling] + others
    for device in greet:
        pl.semaphore_signal(barrier, inc=1, device_id=device, device_id_type=MESH)
    pl.semaphore_wait(barrier, len(greet))

    def remote(src, dst, send, recv, device):
        return pltpu.make_async_remote_copy(
            src_ref=src, dst_ref=dst, send_sem=send, recv_sem=recv,
            device_id=device, device_id_type=MESH,
        )

    def origin_of(distance, d):
        return (z + NZ - distance) % NZ if d == 0 else (z + distance) % NZ

    def chunk(origin, c):
        if c == EXTRA:
            return big.at[q, 1 - xh, origin, pl.ds(0, 1)]
        return big.at[q, xh, origin, pl.ds(CHUNKS[c][0], CHUNKS[c][1])]

    def ring(step, d, c):
        ref = chunk(origin_of(step - 1, d), c)
        return remote(
            ref, ref, send.at[RING if c < EXTRA else RING_X], ring_r.at[d, step - 1, c], along_z(1 if d == 0 else -1)
        )

    def arrival(step, d, c):
        ref = chunk(origin_of(step, d), c)
        return remote(
            ref, ref, send.at[RING if c < EXTRA else RING_X], ring_r.at[d, step - 1, c], along_z(1 if d == 0 else -1)
        )

    def crosses(c):
        return c < EXTRA and sum(CHUNKS[c]) > 1

    def to_sibling(origin, slot, d, c):
        ref = chunk(origin, c)
        return remote(ref, ref, send.at[SIB if c < EXTRA else SIB_X], sib_r.at[2 if c == EXTRA else 1], sibling)

    def to_peer(origin, slot, d, c):
        first = max(CHUNKS[c][0], 1)
        ref = big.at[q, xh, origin, pl.ds(first, sum(CHUNKS[c]) - first)]
        return remote(ref, ref, send.at[X], x_r.at[d, slot], peer)

    def peer_part(origin, part):
        return big.at[q, 1 - xh, origin, part]

    def from_peer(origin, slot, d, part):
        ref = peer_part(origin, part)
        return remote(ref, ref, send.at[SIB_PEER], x_r.at[d, slot], peer)

    def peer_to_sibling(origin, slot, d, part):
        ref = peer_part(origin, part)
        return remote(ref, ref, send.at[SIB_PEER], sib_r.at[3], sibling)

    REST, ONE, TWO = pl.ds(1, 3), pl.ds(1, 1), pl.ds(2, 2)

    def last_leaves(d, c):
        return (d == 1) == (c < EXTRA and CHUNKS[c][0] >= 2)

    LAST = [(d, c) for c in range(EXTRA + 1) for d in (0, 1) if last_leaves(d, c)]

    def take_big(step, d, c, send):
        arrival(step, d, c).wait_recv()
        if send:
            ring(step + 1, d, c).start()
        origin = origin_of(step, d)
        if crosses(c):
            to_peer(origin, step, d, c).start()
        to_sibling(origin, step, d, c).start()

    def peer_arrivals(step):
        for d in (0, 1):
            origin = origin_of(step, d)
            from_peer(origin, step, d, REST).wait_recv()
            peer_to_sibling(origin, step, d, REST).start()

    def small_part(parity, origin, h):
        return small.at[q, parity, origin, h]

    def tree(held, hop, d, h):
        ref = small_part(par, origin_of(held, d), h)
        to = held + hop - 1
        return remote(ref, ref, send.at[TREE], tree_r.at[d, to, h], along_z(hop if d == 0 else -hop))

    def small_arrival(distance, d, h):
        ref = small_part(par, origin_of(distance, d), h)
        return remote(ref, ref, send.at[TREE], tree_r.at[d, distance - 1, h], along_z(1))

    def small_to_y(distance, d, h):
        ref = small_part(par, origin_of(distance, d), h)
        return remote(ref, ref, send.at[Y], y_r.at[d, distance, h], along_y(1 if h == 0 else -1))

    def small_to_sibling(distance, d, h):
        ref = small_part(par, origin_of(distance, d), h)
        return remote(ref, ref, send.at[SIB_SMALL], sib_r.at[0], sibling)

    def y_arrival(distance, d, h):
        ref = small_part(1 - par, origin_of(distance, d), h)
        return remote(ref, ref, send.at[Y], y_r.at[d, distance, h], sibling)

    def y_to_sibling(distance, d, h):
        ref = small_part(1 - par, origin_of(distance, d), h)
        return remote(ref, ref, send.at[SIB_SMALL], sib_r.at[0], sibling)

    def take_small(distance, even, last, d, h):
        small_arrival(distance, d, h).wait_recv()
        if even:
            if not last or h == d:
                tree(distance, 2, d, h).start()
            tree(distance, 1, d, h).start()
        small_to_y(distance, d, h).start()
        small_to_sibling(distance, d, h).start()

    def take_y(distance, d, h):
        y_arrival(distance, d, h).wait_recv()
        y_to_sibling(distance, d, h).start()

    def chain(k):
        parity, slot = BLOCK[(0, k)]
        src = fac.at[pl.ds(0, k), :, pl.ds(0, NB)]
        dst = small.at[q, parity, z, xh, pl.ds(slot, k)]
        return src, dst

    def inverse_part(parity, h):
        src = inv.at[pl.ds(0, 3)] if parity == 0 else inv.at[pl.ds(3, 1)]
        dst = small.at[q, parity, z, h, pl.ds(2, 3) if parity == 0 else pl.ds(4, 1)]
        return src, dst

    for k in (1, 2, 3):

        @pl.when(row == k)
        def _(k=k):
            src, dst = chain(k)
            for i, device in enumerate(alike):
                remote(src, dst, ch_s.at[i], ch_r.at[k - 1, xh], device).start()
            pltpu.make_async_copy(src, dst, ch_r.at[k - 1, xh]).start()

    for parity in (0, 1):

        @pl.when(par == parity)
        def _(parity=parity):
            src, dst = inverse_part(parity, xh)
            remote(src, dst, ch_s.at[7], ch_r.at[3, 0], peer).start()
            pltpu.make_async_copy(src, dst, ch_r.at[3, 1]).start()

    def b_half(ref, part):
        return ref.at[pl.ds(part * HALF, HALF)]

    def b_cross(k, part):
        return remote(
            b_half(rs_hbm, part), b_half(bvec.at[k], part), b_s.at[3, part], b_r.at[k, part], at(k + 4, xh, z, q)
        )

    for k in range(OWNERS):

        @pl.when(row == k)
        def _(k=k):
            for part in (0, 1):
                b_cross(k, part).start()

    own_big.wait()
    own_panel = big.at[q, xh, z, pl.ds(0, 1)]
    panel_out = remote(own_panel, own_panel, send.at[PANEL], p_r.at[0], peer)
    panel_out.start()
    for c in range(EXTRA):
        for d in (0, 1):
            ring(1, d, c).start()
    for c in range(EXTRA):
        if crosses(c):
            to_peer(z, 0, 0, c).start()
        to_sibling(z, 0, 0, c).start()

    for k in range(OWNERS):

        @pl.when(row == k)
        def _(k=k):
            for part in (0, 1):
                for i, hop in enumerate((1, -1, 2)):
                    remote(
                        b_half(rs_hbm, part), b_half(bvec.at[k], part), b_s.at[i, part], b_r.at[k, part], along_y(hop)
                    ).start()
                pltpu.make_async_copy(
                    b_half(rs_hbm, part), b_half(bvec.at[k], part), b_r.at[k, part]
                ).start()

    def b_wait(k, part):
        pltpu.make_async_copy(b_half(rs_hbm, part), b_half(bvec.at[k], part), b_r.at[k, part]).wait()

    def forward_b(part):
        for k in range(OWNERS):

            @pl.when(row == OWNERS + k)
            def _(k=k):
                b_wait(k, part)
                ref = b_half(bvec.at[k], part)
                for i, hop in enumerate((1, -1, 2)):
                    remote(ref, ref, b_s.at[i, part], b_r.at[k, part], along_y(hop)).start()

    peer_panel = big.at[q, 1 - xh, z, pl.ds(0, 1)]
    remote(peer_panel, peer_panel, send.at[PANEL], p_r.at[0], peer).wait_recv()
    for d in (0, 1):
        ring(1, d, EXTRA).start()
    to_sibling(z, 0, 0, EXTRA).start()

    for c in range(EXTRA):
        for d in (0, 1):
            take_big(1, d, c, True)

    for parity in (0, 1):

        @pl.when(par == parity)
        def _(parity=parity):
            for sem, h in ((ch_r.at[3, 1], xh), (ch_r.at[3, 0], 1 - xh)):
                src, dst = inverse_part(parity, h)
                pltpu.make_async_copy(src, dst, sem).wait()
            for k in (2,) if parity == 0 else (1, 3):
                for h in (0, 1):
                    ref = small.at[q, parity, z, h, pl.ds(BLOCK[(0, k)][1], k)]
                    pltpu.make_async_copy(ref, ref, ch_r.at[k - 1, h]).wait()

    for h in (0, 1):
        for d in (0, 1):
            tree(0, 2, d, h).start()
            tree(0, 1, d, h).start()
        small_to_y(0, 0, h).start()
        small_to_sibling(0, 0, h).start()

    for d in (0, 1):
        take_big(1, d, EXTRA, True)
    from_peer(z, 0, 0, REST).wait_recv()
    peer_to_sibling(z, 0, 0, REST).start()

    def big_step(step):
        for c in range(EXTRA + 1):
            for d in (0, 1):
                take_big(step, d, c, True)
        if step > 2:
            peer_arrivals(step - 2)

    big_step(2)
    forward_b(0)

    def steps(j, carry):
        for h in (0, 1):
            for d in (0, 1):
                small_arrival(2 * j, d, h).wait_recv()
                if h == d:
                    tree(2 * j, 2, d, h).start()
                else:

                    @pl.when(j < 3)
                    def _(d=d, h=h):
                        tree(2 * j, 2, d, h).start()

                tree(2 * j, 1, d, h).start()
                small_to_y(2 * j, d, h).start()
                small_to_sibling(2 * j, d, h).start()
        for h in (0, 1):
            for d in (0, 1):
                take_small(2 * j - 1, False, False, d, h)

        @pl.when(j == 1)
        def _():
            forward_b(1)
            for h in (0, 1):
                take_y(0, 0, h)

        @pl.when(j > 1)
        def _():
            for h in (0, 1):
                for d in (0, 1):
                    take_y(2 * j - 3, d, h)
                    take_y(2 * j - 2, d, h)

        for c in range(EXTRA + 1):
            for d in (0, 1):
                take_big(j + 2, d, c, True)
        peer_arrivals(j + 0)
        return carry

    lax.fori_loop(1, 4, steps, 0)
    for h in (0, 1):
        take_small(8, False, False, h, h)
    for h in (0, 1):
        for d in (0, 1):
            take_small(7, False, False, d, h)
    for h in (0, 1):
        for d in (0, 1):
            take_y(5, d, h)
            take_y(6, d, h)
    for c in range(EXTRA + 1):
        for d in (0, 1):
            take_big(6, d, c, True)
    peer_arrivals(4)
    for h in (0, 1):
        take_y(8, h, h)
        for d in (0, 1):
            take_y(7, d, h)

    for c in range(EXTRA + 1):
        for d in (0, 1):
            take_big(7, d, c, last_leaves(d, c))
    peer_arrivals(5)

    sib_small = small.at[1 - q]
    pltpu.make_async_copy(sib_small, sib_small, sib_r.at[0]).wait()

    def prepare(place, carry):
        parity, slot = place // SLOTS, place % SLOTS
        for half in (0, 1):
            value = jnp.concatenate(
                [small[0, parity, :, half, slot], small[1, parity, :, half, slot]], axis=1
            ).reshape(HALF, NB)
            ahi[place, pl.ds(half * HALF, HALF), :], alo[place, pl.ds(half * HALF, HALF), :] = split(value)
        return carry

    lax.fori_loop(0, 2 * SLOTS, prepare, 0)
    load_rs.wait()

    def solve(k, carry):
        @pl.when(row != OWNERS + k)
        def _():
            for part in (0, 1):
                b_wait(k, part)

        def reduce(m, work):
            place = m + (k % 2) * (5 + k // 2)
            x = tuple(ref[m].reshape(NB, NB) for ref in (xhi, xlo))
            return work - dot3((ahi[place], alo[place]), x, ((0,), (0,)))

        work = lax.fori_loop(0, k, reduce, bvec[k])
        place = 2 + k + 4 * (k // 3)
        answer = dot3((ahi[place], alo[place]), split(work), ((1,), (0,)))

        @pl.when(row == k)
        def _():
            out[pl.ds(0, NB), :] = answer

        high, low = split(answer)
        xhi[k] = high.reshape(2, HALF, NB)
        xlo[k] = low.reshape(2, HALF, NB)

        @pl.when(k == 0)
        def _():
            for d, c in LAST:
                take_big(8, d, c, False)
            peer_arrivals(6)

        @pl.when(k == 2)
        def _():
            peer_arrivals(7)

        return carry

    lax.fori_loop(0, PANELS, solve, 0)
    for d, part in ((0, ONE), (1, TWO)):
        origin = origin_of(8, d)
        from_peer(origin, 8, d, part).wait_recv()
        peer_to_sibling(origin, 8, d, part).start()

    def update(block, parts):
        lanes = pl.ds(pl.multiple_of(block * NB, NB), NB)

        def factor(half, k):
            return jnp.concatenate(
                [big[0, half, :, k, :, lanes], big[1, half, :, k, :, lanes]], axis=1
            ).reshape(HALF, NB)

        total = None
        for group in parts:
            f = jnp.concatenate([factor(half, k) for half, k in group], axis=0)
            x = tuple(
                jnp.concatenate([ref[k, half] for half, k in group], axis=0) for ref in (xhi, xlo)
            )
            term = dot3(split(f), x, ((0,), (0,)))
            total = term if total is None else total + term
        rows = pl.ds(pl.multiple_of(block * NB, NB), NB)
        out[rows, :] = out[rows, :] - total

    def all_blocks(parts):
        def blocks(block, carry):
            update(block, parts)
            return carry

        lax.fori_loop(1 - row // OWNERS, 4, blocks, 0)

    own_half = big.at[1 - q, xh]
    pltpu.make_async_copy(own_half, own_half, sib_r.at[1]).wait()
    one_panel = big.at[1 - q, 1 - xh, :, pl.ds(0, 1)]
    pltpu.make_async_copy(one_panel, one_panel, sib_r.at[2]).wait()
    all_blocks((((xh, 0), (xh, 1)), ((xh, 2), (xh, 3)), ((1 - xh, 0),)))
    rest = big.at[1 - q, 1 - xh, :, REST]
    pltpu.make_async_copy(rest, rest, sib_r.at[3]).wait()
    all_blocks((((1 - xh, 1), (1 - xh, 2)), ((1 - xh, 3),)))

    def left(kind, ref):
        pltpu.make_async_copy(ref, ref, send.at[kind]).wait()

    most = pl.ds(0, NZ - 1)
    left(PANEL, own_panel)
    left(RING, big.at[q, xh, most])
    left(RING_X, big.at[q, 1 - xh, most, pl.ds(0, 1)])
    left(TREE, small.at[q, par, most])
    left(Y, small.at[q, par])
    left(X, big.at[q, xh, :, REST])
    left(SIB, big.at[q, xh])
    left(SIB_X, big.at[q, 1 - xh, :, pl.ds(0, 1)])
    left(SIB_SMALL, small.at[q])
    left(SIB_PEER, big.at[q, 1 - xh, :, REST])

    for k in (1, 2, 3):

        @pl.when(row == k)
        def _(k=k):
            src, dst = chain(k)
            for i, device in enumerate(alike):
                remote(src, dst, ch_s.at[i], ch_r.at[k - 1, xh], device).wait_send()

    for parity in (0, 1):

        @pl.when(par == parity)
        def _(parity=parity):
            src, dst = inverse_part(parity, xh)
            remote(src, dst, ch_s.at[7], ch_r.at[3, 0], peer).wait_send()

    for part in (0, 1):
        ref = b_half(bvec.at[0], part)
        for i in range(3):
            remote(ref, ref, b_s.at[i, part], b_r.at[0, part], peer).wait_send()

    @pl.when(row < OWNERS)
    def _():
        for part in (0, 1):
            b_cross(0, part).wait_send()


def per_device(right_side, factor_panels, inverses):
    rows, columns = right_side.shape
    dma = pltpu.SemaphoreType.DMA
    return pl.pallas_call(
        kernel,
        name="solve",
        out_shape=pltpu.VMEM((rows, columns), F32),
        in_specs=[pl.BlockSpec(memory_space=pltpu.HBM)] * 3,
        out_specs=pl.BlockSpec(memory_space=pltpu.VMEM),
        scratch_shapes=[
            pltpu.VMEM((2, 2, NZ, PANELS, 4, rows), F32),
            pltpu.VMEM((2, 2, NZ, 2, SLOTS, 4, NB), F32),
            pltpu.VMEM((OWNERS, NB, columns), F32),
            pltpu.VMEM((PANELS, 2, HALF, columns), BF16),
            pltpu.VMEM((PANELS, 2, HALF, columns), BF16),
            pltpu.VMEM((2 * SLOTS, NB, NB), BF16),
            pltpu.VMEM((2 * SLOTS, NB, NB), BF16),
            dma((10,)),
            dma((2, 8, EXTRA + 1)),
            dma((2, 8, 2)),
            dma((2, 9, 2)),
            dma((2, 9)),
            dma((1,)),
            dma((4,)),
            dma((8,)),
            dma((4, 2)),
            dma((4, 2)),
            dma((4, 2)),
            dma((2,)),
        ],
        compiler_params=pltpu.CompilerParams(
            collective_id=0, has_side_effects=True, vmem_limit_bytes=62 << 20
        ),
        cost_estimate=pl.CostEstimate(flops=1 << 31, bytes_accessed=8 << 20, transcendentals=0),
    )(right_side, factor_panels, inverses)


def solution(mesh):
    in_specs = (P("row", "col"), P(None, "col", "row"), P(None, "col", None))
    return jax.shard_map(
        per_device, mesh=mesh, in_specs=in_specs, out_specs=P("row", "col"), check_vma=False
    )
```

time: 671 us -> 61.8 us (0.09)
  waiting for transfers between devices: 325 us -> 0 us
  blocking collectives: 308 us -> 0 us
  Pallas kernels: 0 us -> 60.8 us
  between operations: 15 us -> 0.01 us
  matrix products: 14.9 us -> 0 us
    all_gather x4 -> x0, blocking collectives: 308 us -> none  [solve_block(): inverse = lax.all_gather(inverses[panel], 'col', axis=0, tiled=True)]
    all_gather x4 -> x0, waiting for transfers between devices: 238 us -> none  [per_device(): lax.all_gather(factor_panels[panel], 'col', axis=0, tiled=True)]
    psum x4 -> x0, waiting for transfers between devices: 86.2 us -> none  [spread(): return lax.psum(jnp.where(mine, value, jnp.zeros_like(value)), axis)]
    pallas_call x0 -> x1, Pallas kernels: none -> 60.8 us  [per_device(): pl.pallas_call(kernel, name='solve', out_shape=pltpu.VMEM((rows, columns)...]
    dot_general x8 -> x0, matrix products: 14.9 us -> none  [the longest x4 9.52 us: contract(): lax.dot_general(factor_rows, answer, (((0,), (0,)), ((), ())), precision=...]
  transfers between devices with their start and end apart: 8 -> 0, of which waited for: 7 -> 0; matrix products, arithmetic and copies ran while one was open for 1% -> 0% of each run, Pallas kernels for 0% -> 0%
where the time goes in v2:
time: 61.8 us; the launch traced here: 61.7 us
  Pallas kernels  60.8 us (98%)
  local copies, waits for them, and re-layouts  0.97 us (2%)
    pallas_call x1, Pallas kernels, per_device(): pl.pallas_call(kernel, name='solve', out_shape=pltpu.VMEM((rows, columns)...  60.8 us

profile of v2, /device:TPU:1, one launch (start us, length us, event | category | flops | bytes accessed | tf_op | source)
XLA Modules:
  0.0 61.7 jit_solution(8615775246617537545)
XLA Ops:
  0.0 60.8 %solve.1 = f32[1024,256]{1,0:T(8,128)S(1)} custom-call(f32[1024,256]{1,0:T(8,128)} %rs_hbm.1, f32[4,4,1024]{2,1,0:T(4,128)} %fac.1, f32[4,4,256]{2,1,0:T(4,128)} %inv.1), custom_call_target="tpu_custom_call" | custom-call | flops 2147483648 | bytes 8388608 | tf_op jit(solution)/shard_map/solve/pallas_call | solution.py:510
  60.8 1.0 %copy.5 = f32[1024,256]{1,0:T(8,128)} copy(f32[1024,256]{1,0:T(8,128)S(1)} %solve.1) | data formatting | bytes 2097152

commit v3 on v2

v3 whole, which is shorter than its diff:
```python
import jax
import jax.numpy as jnp
from jax import lax
from jax.experimental import pallas as pl
from jax.experimental.pallas import tpu as pltpu
from jax.sharding import PartitionSpec as P

MESH = pl.DeviceIdType.MESH
NZ = 16
PANELS = 4
OWNERS = 4
NB = 256
HALF = 128
CHUNKS = ((0, 2), (2, 2))
SLOTS = 3
BF16 = jnp.bfloat16
F32 = jnp.float32

def block_place(m, k):
    return SLOTS * k + m


def inverse_place(k):
    return k + k // 3


RING, TREE, Y, RELAY, X, SIB, SIB_SMALL, SIB_PEER = range(8)


def split(value):
    high = value.astype(BF16)
    low = (value - high.astype(F32)).astype(BF16)
    return high, low


def dot3(a, b, dims):
    def one(p, q):
        return lax.dot_general(p, q, (dims, ((), ())), preferred_element_type=F32)

    return one(a[0], b[0]) + (one(a[0], b[1]) + one(a[1], b[0]))


def kernel(
    rs_hbm, fac, inv, out,
    big, small, bvec, xhi, xlo, ahi, alo,
    send, ring_r, tree_r, y_r, x_r, sib_r,
    ch_s, ch_r, b_s, b_r, loc_s,
):
    row = lax.axis_index("row")
    col = lax.axis_index("col")
    y = row % 4
    xh, z, q = col // 32, (col // 2) % NZ, col % 2

    def at(row_to, xh_to, z_to, q_to):
        return (row_to, (xh_to * NZ + z_to) * 2 + q_to)

    def along_z(hop):
        return at(row, xh, (z + NZ + hop) % NZ, q)

    def along_y(hop):
        return at((row // 4) * 4 + (y + 4 + hop) % 4, xh, z, q)

    sibling = at(row, xh, z, 1 - q)
    peer = at(row, 1 - xh, z, q)
    alike = [at((row + 4 * (i % 2)) % 8, (xh + i // 2) % 2, z, q) for i in (1, 2, 3)]
    across_y = [along_y(1), along_y(-1)]
    before, after, over = (y + 3) % 4, (y + 1) % 4, (y + 2) % 4

    own_big = pltpu.make_async_copy(fac, big.at[q, xh, z], loc_s.at[1])
    own_big.start()
    load_rs = pltpu.make_async_copy(rs_hbm, out, loc_s.at[0])
    load_rs.start()

    barrier = pltpu.get_barrier_semaphore()
    greet = [along_z(hop) for hop in (1, -1, 2, -2)] + [sibling] + alike + across_y
    for device in greet:
        pl.semaphore_signal(barrier, inc=1, device_id=device, device_id_type=MESH)
    pl.semaphore_wait(barrier, len(greet))

    def remote(src, dst, send, recv, device):
        return pltpu.make_async_remote_copy(
            src_ref=src, dst_ref=dst, send_sem=send, recv_sem=recv,
            device_id=device, device_id_type=MESH,
        )

    def origin_of(distance, d):
        return (z + NZ - distance) % NZ if d == 0 else (z + distance) % NZ

    def chunk(origin, c):
        return big.at[q, xh, origin, pl.ds(CHUNKS[c][0], CHUNKS[c][1])]

    def hop_to(hop, d):
        return along_z(hop if d == 0 else -hop)

    def grow(held, hop, d, c):
        ref = chunk(origin_of(held, d), c)
        return remote(ref, ref, send.at[RING], ring_r.at[d, held + hop - 1, c], hop_to(hop, d))

    def arrival(distance, d, c):
        ref = chunk(origin_of(distance, d), c)
        return remote(ref, ref, send.at[RING], ring_r.at[d, distance - 1, c], hop_to(1, d))

    def to_sibling(origin, slot, d, c):
        ref = chunk(origin, c)
        return remote(ref, ref, send.at[SIB], sib_r.at[1], sibling)

    def to_peer(origin, slot, d, c):
        ref = chunk(origin, c)
        return remote(ref, ref, send.at[X], x_r.at[d, slot], peer)

    def peer_part(origin, part):
        return big.at[q, 1 - xh, origin, part]

    def from_peer(origin, slot, d, part):
        ref = peer_part(origin, part)
        return remote(ref, ref, send.at[SIB_PEER], x_r.at[d, slot], peer)

    def peer_to_sibling(origin, slot, d, part):
        ref = peer_part(origin, part)
        return remote(ref, ref, send.at[SIB_PEER], sib_r.at[3], sibling)

    REST, ONE, TWO = pl.ds(0, 4), pl.ds(0, 2), pl.ds(2, 2)

    def last_leaves(d, c):
        return (d == 1) == (CHUNKS[c][0] >= 2)

    LAST = [(d, c) for c in range(len(CHUNKS)) for d in (0, 1) if last_leaves(d, c)]

    def hand_on(distance, d, c):
        origin = origin_of(distance, d)
        to_peer(origin, distance, d, c).start()
        to_sibling(origin, distance, d, c).start()

    def take_end(distance, d, c):
        arrival(distance, d, c).wait_recv()
        hand_on(distance, d, c)

    def peer_arrivals(step):
        for d in (0, 1):
            origin = origin_of(step, d)
            from_peer(origin, step, d, REST).wait_recv()
            peer_to_sibling(origin, step, d, REST).start()

    def small_part(quarter, origin, h):
        return small.at[q, quarter, origin, h]

    def tree(held, hop, d, h):
        ref = small_part(y, origin_of(held, d), h)
        to = held + hop - 1
        return remote(ref, ref, send.at[TREE], tree_r.at[d, to, h], along_z(hop if d == 0 else -hop))

    def small_arrival(distance, d, h):
        ref = small_part(y, origin_of(distance, d), h)
        return remote(ref, ref, send.at[TREE], tree_r.at[d, distance - 1, h], along_z(1))

    def small_to_y(distance, d, h, i):
        ref = small_part(y, origin_of(distance, d), h)
        return remote(ref, ref, send.at[Y], y_r.at[i, d, distance, h], across_y[i])

    def small_to_sibling(distance, d, h):
        ref = small_part(y, origin_of(distance, d), h)
        return remote(ref, ref, send.at[SIB_SMALL], sib_r.at[0], sibling)

    def y_arrival(distance, d, h, i):
        ref = small_part((before, after, over)[i], origin_of(distance, d), h)
        return remote(ref, ref, send.at[SIB_SMALL], y_r.at[i, d, distance, h], sibling)

    def y_to_sibling(distance, d, h, i):
        ref = small_part((before, after, over)[i], origin_of(distance, d), h)
        return remote(ref, ref, send.at[SIB_SMALL], sib_r.at[0], sibling)

    def relay(distance, d, h):
        ref = small_part((before, after)[h], origin_of(distance, d), h)
        return remote(ref, ref, send.at[RELAY], y_r.at[2, d, distance, h], across_y[h])

    def spread(distance, d, h):
        for i in (0, 1):
            small_to_y(distance, d, h, i).start()
        small_to_sibling(distance, d, h).start()

    def take_odd(distance, d, h):
        small_arrival(distance, d, h).wait_recv()
        spread(distance, d, h)

    def take_y(distance, d, h):
        for i in (0, 1):
            y_arrival(distance, d, h, i).wait_recv()
            if i == h:
                relay(distance, d, h).start()
            y_to_sibling(distance, d, h, i).start()

    def take_over(distance, d, h):
        y_arrival(distance, d, h, 2).wait_recv()
        y_to_sibling(distance, d, h, 2).start()

    def chain(k, h):
        return fac.at[pl.ds(0, k), :, pl.ds(0, NB)], small.at[q, k, z, h, pl.ds(0, k)]

    for k in (1, 2, 3):

        @pl.when(row == k)
        def _(k=k):
            src, dst = chain(k, xh)
            for i, device in enumerate(alike):
                remote(src, dst, ch_s.at[i], ch_r.at[xh], device).start()
            pltpu.make_async_copy(src, dst, ch_r.at[xh]).start()

    def inverse_part(quarter, h):
        src = inv.at[pl.ds(0, 3)] if quarter == 0 else inv.at[pl.ds(3, 1)]
        return src, small.at[q, quarter, z, h, pl.ds(0, 3) if quarter == 0 else pl.ds(1, 1)]

    for quarter in (0, 1):

        @pl.when(y == quarter)
        def _(quarter=quarter):
            src, dst = inverse_part(quarter, xh)
            remote(src, dst, ch_s.at[3], ch_r.at[2], peer).start()
            pltpu.make_async_copy(src, dst, ch_r.at[3]).start()

    @pl.when((y == 1) | (y == 2))
    def _():
        for h in (0, 1):
            small[q, y, z, h, 2] = jnp.zeros((4, NB), F32)

    def b_half(ref, part):
        return ref.at[pl.ds(part * HALF, HALF)]

    def b_cross(k, part):
        return remote(
            b_half(rs_hbm, part), b_half(bvec.at[k], part), b_s.at[3, part], b_r.at[k, part], at(k + 4, xh, z, q)
        )

    for k in range(OWNERS):

        @pl.when(row == k)
        def _(k=k):
            for part in (0, 1):
                b_cross(k, part).start()

    own_big.wait()
    for c in range(len(CHUNKS)):
        for d in (0, 1):
            grow(0, 2, d, c).start()
            grow(0, 1, d, c).start()
    for c in range(len(CHUNKS)):
        to_peer(z, 0, 0, c).start()
        to_sibling(z, 0, 0, c).start()

    for k in range(OWNERS):

        @pl.when(row == k)
        def _(k=k):
            for part in (0, 1):
                for i in (0, 1):
                    remote(
                        b_half(rs_hbm, part), b_half(bvec.at[k], part), b_s.at[i, part], b_r.at[k, part], across_y[i]
                    ).start()
                pltpu.make_async_copy(
                    b_half(rs_hbm, part), b_half(bvec.at[k], part), b_r.at[k, part]
                ).start()

    def b_wait(k, part):
        pltpu.make_async_copy(b_half(rs_hbm, part), b_half(bvec.at[k], part), b_r.at[k, part]).wait()

    def forward_b(part):
        for k in range(OWNERS):

            @pl.when(row == OWNERS + k)
            def _(k=k):
                b_wait(k, part)
                ref = b_half(bvec.at[k], part)
                for i in (0, 1):
                    remote(ref, ref, b_s.at[i, part], b_r.at[k, part], across_y[i]).start()

    def relay_b(part):
        k = (before, after)[part]
        b_wait(k, part)
        ref = b_half(bvec.at[k], part)
        remote(ref, ref, b_s.at[2, part], b_r.at[k, part], across_y[part]).start()

    for quarter in (0, 1):

        @pl.when(y == quarter)
        def _(quarter=quarter):
            for sem, h in ((ch_r.at[3], xh), (ch_r.at[2], 1 - xh)):
                src, dst = inverse_part(quarter, h)
                pltpu.make_async_copy(src, dst, sem).wait()

    for k in (1, 2, 3):

        @pl.when(y == k)
        def _(k=k):
            for h in (0, 1):
                src, dst = chain(k, h)
                pltpu.make_async_copy(src, dst, ch_r.at[h]).wait()

    for h in (0, 1):
        for d in (0, 1):
            tree(0, 2, d, h).start()
            tree(0, 1, d, h).start()
        spread(0, 0, h)

    def steps(j, carry):
        for c in range(len(CHUNKS)):
            for d in (0, 1):
                arrival(2 * j, d, c).wait_recv()
                if last_leaves(d, c):
                    grow(2 * j, 2, d, c).start()
                else:

                    @pl.when(j < 3)
                    def _(d=d, c=c):
                        grow(2 * j, 2, d, c).start()

                grow(2 * j, 1, d, c).start()
                hand_on(2 * j, d, c)
        for h in (0, 1):
            for d in (0, 1):
                small_arrival(2 * j, d, h).wait_recv()
                if h == d:
                    tree(2 * j, 2, d, h).start()
                else:

                    @pl.when(j < 3)
                    def _(d=d, h=h):
                        tree(2 * j, 2, d, h).start()

                tree(2 * j, 1, d, h).start()
                spread(2 * j, d, h)
        for h in (0, 1):
            for d in (0, 1):
                take_odd(2 * j - 1, d, h)

        for c in range(len(CHUNKS)):
            for d in (0, 1):
                take_end(2 * j - 1, d, c)

        @pl.when(j == 1)
        def _():
            from_peer(z, 0, 0, REST).wait_recv()
            peer_to_sibling(z, 0, 0, REST).start()
            forward_b(0)
            for h in (0, 1):
                take_y(0, 0, h)

        @pl.when(j > 1)
        def _():
            for h in (0, 1):
                for d in (0, 1):
                    take_y(2 * j - 3, d, h)
                    take_y(2 * j - 2, d, h)
            peer_arrivals(2 * j - 3)
            peer_arrivals(2 * j - 2)

        @pl.when(j == 2)
        def _():
            forward_b(1)
            for h in (0, 1):
                take_over(0, 0, h)

        @pl.when(j == 3)
        def _():
            for part in (0, 1):
                relay_b(part)
            for h in (0, 1):
                for d in (0, 1):
                    take_over(1, d, h)
                    take_over(2, d, h)

        return carry

    lax.fori_loop(1, 4, steps, 0)
    for d, c in LAST:
        take_end(8, d, c)
    for h in (0, 1):
        take_odd(8, h, h)
    for h in (0, 1):
        for d in (0, 1):
            take_odd(7, d, h)
    for c in range(len(CHUNKS)):
        for d in (0, 1):
            take_end(7, d, c)
    for h in (0, 1):
        for d in (0, 1):
            take_y(5, d, h)
            take_y(6, d, h)
            take_over(3, d, h)
            take_over(4, d, h)
    peer_arrivals(5)
    peer_arrivals(6)
    for h in (0, 1):
        take_y(8, h, h)
        for d in (0, 1):
            take_y(7, d, h)
            take_over(5, d, h)
            take_over(6, d, h)
    for h in (0, 1):
        take_over(8, h, h)
        for d in (0, 1):
            take_over(7, d, h)

    sib_small = small.at[1 - q]
    pltpu.make_async_copy(sib_small, sib_small, sib_r.at[0]).wait()

    @pl.when(row < OWNERS)
    def _():
        for part in (0, 1):
            b_wait(y, part)

    b_wait(before, 1)
    b_wait(after, 0)
    for part in (0, 1):
        b_wait(over, part)

    def prepare(place, carry):
        quarter, slot = place // SLOTS, place % SLOTS
        for half in (0, 1):
            value = jnp.concatenate(
                [small[0, quarter, :, half, slot], small[1, quarter, :, half, slot]], axis=1
            ).reshape(HALF, NB)
            ahi[place, pl.ds(half * HALF, HALF), :], alo[place, pl.ds(half * HALF, HALF), :] = split(value)
        return carry

    lax.fori_loop(0, 5, prepare, 0)
    lax.fori_loop(6, 8, prepare, 0)
    lax.fori_loop(9, 12, prepare, 0)
    load_rs.wait()

    work = [bvec[k] for k in range(PANELS)]
    for k in range(PANELS):
        place = inverse_place(k)
        answer = dot3((ahi[place], alo[place]), split(work[k]), ((1,), (0,)))
        x = split(answer)
        for m in range(k + 1, PANELS):
            place = block_place(k, m)
            work[m] = work[m] - dot3((ahi[place], alo[place]), x, ((0,), (0,)))

        @pl.when(row == k)
        def _(answer=answer):
            out[pl.ds(0, NB), :] = answer

        xhi[k] = x[0].reshape(2, HALF, NB)
        xlo[k] = x[1].reshape(2, HALF, NB)
        if k == 1:
            peer_arrivals(7)
    for d, part in ((0, ONE), (1, TWO)):
        origin = origin_of(8, d)
        from_peer(origin, 8, d, part).wait_recv()
        peer_to_sibling(origin, 8, d, part).start()

    def update(block, parts):
        lanes = pl.ds(pl.multiple_of(block * NB, NB), NB)

        def factor(half, k):
            return jnp.concatenate(
                [big[0, half, :, k, :, lanes], big[1, half, :, k, :, lanes]], axis=1
            ).reshape(HALF, NB)

        total = None
        for group in parts:
            f = jnp.concatenate([factor(half, k) for half, k in group], axis=0)
            x = tuple(
                jnp.concatenate([ref[k, half] for half, k in group], axis=0) for ref in (xhi, xlo)
            )
            term = dot3(split(f), x, ((0,), (0,)))
            total = term if total is None else total + term
        rows = pl.ds(pl.multiple_of(block * NB, NB), NB)
        out[rows, :] = out[rows, :] - total

    def all_blocks(parts):
        def blocks(block, carry):
            update(block, parts)
            return carry

        lax.fori_loop(1 - row // OWNERS, 4, blocks, 0)

    own_half = big.at[1 - q, xh]
    pltpu.make_async_copy(own_half, own_half, sib_r.at[1]).wait()
    all_blocks((((xh, 0), (xh, 1)), ((xh, 2), (xh, 3))))
    rest = big.at[1 - q, 1 - xh, :, REST]
    pltpu.make_async_copy(rest, rest, sib_r.at[3]).wait()
    all_blocks((((1 - xh, 0), (1 - xh, 1)), ((1 - xh, 2), (1 - xh, 3))))

    def left(kind, ref):
        pltpu.make_async_copy(ref, ref, send.at[kind]).wait()

    most = pl.ds(0, NZ - 1)
    left(RING, big.at[q, xh, most])
    left(TREE, small.at[q, y, most])
    left(Y, small.at[q, pl.ds(0, 2)])
    left(RELAY, small.at[q, 0])
    left(X, big.at[q, xh, :, REST])
    left(SIB, big.at[q, xh])
    left(SIB_SMALL, small.at[q])
    left(SIB_PEER, big.at[q, 1 - xh, :, REST])

    for k in (1, 2, 3):

        @pl.when(row == k)
        def _(k=k):
            src, dst = chain(k, xh)
            for i, device in enumerate(alike):
                remote(src, dst, ch_s.at[i], ch_r.at[xh], device).wait_send()

    for quarter in (0, 1):

        @pl.when(y == quarter)
        def _(quarter=quarter):
            src, dst = inverse_part(quarter, xh)
            remote(src, dst, ch_s.at[3], ch_r.at[2], peer).wait_send()

    for part in (0, 1):
        ref = b_half(bvec.at[0], part)
        for i in range(3):
            remote(ref, ref, b_s.at[i, part], b_r.at[0, part], peer).wait_send()

    @pl.when(row < OWNERS)
    def _():
        for part in (0, 1):
            b_cross(0, part).wait_send()


def per_device(right_side, factor_panels, inverses):
    rows, columns = right_side.shape
    dma = pltpu.SemaphoreType.DMA
    return pl.pallas_call(
        kernel,
        name="solve",
        out_shape=pltpu.VMEM((rows, columns), F32),
        in_specs=[pl.BlockSpec(memory_space=pltpu.HBM)] * 3,
        out_specs=pl.BlockSpec(memory_space=pltpu.VMEM),
        scratch_shapes=[
            pltpu.VMEM((2, 2, NZ, PANELS, 4, rows), F32),
            pltpu.VMEM((2, 4, NZ, 2, SLOTS, 4, NB), F32),
            pltpu.VMEM((OWNERS, NB, columns), F32),
            pltpu.VMEM((PANELS, 2, HALF, columns), BF16),
            pltpu.VMEM((PANELS, 2, HALF, columns), BF16),
            pltpu.VMEM((4 * SLOTS, NB, NB), BF16),
            pltpu.VMEM((4 * SLOTS, NB, NB), BF16),
            dma((8,)),
            dma((2, 8, len(CHUNKS))),
            dma((2, 8, 2)),
            dma((3, 2, 9, 2)),
            dma((2, 9)),
            dma((4,)),
            dma((4,)),
            dma((4,)),
            dma((4, 2)),
            dma((4, 2)),
            dma((2,)),
        ],
        compiler_params=pltpu.CompilerParams(
            collective_id=0, has_side_effects=True, vmem_limit_bytes=62 << 20
        ),
        cost_estimate=pl.CostEstimate(flops=1 << 31, bytes_accessed=8 << 20, transcendentals=0),
    )(right_side, factor_panels, inverses)


def solution(mesh):
    in_specs = (P("row", "col"), P(None, "col", "row"), P(None, "col", None))
    return jax.shard_map(
        per_device, mesh=mesh, in_specs=in_specs, out_specs=P("row", "col"), check_vma=False
    )
```

time: 61.8 us -> 57.1 us (0.924)
  Pallas kernels: 60.8 us -> 56 us
    pallas_call x1, Pallas kernels: 60.8 us -> 56 us  [per_device(): pl.pallas_call(kernel, name='solve', out_shape=pltpu.VMEM((rows, columns)...]
where the time goes in v3:
time: 57.1 us; the launch traced here: 57 us
  Pallas kernels  56 us (98%)
  local copies, waits for them, and re-layouts  0.97 us (2%)
    pallas_call x1, Pallas kernels, per_device(): pl.pallas_call(kernel, name='solve', out_shape=pltpu.VMEM((rows, columns)...  56 us

profile of v3, /device:TPU:1, one launch (start us, length us, event | category | flops | bytes accessed | tf_op | source)
XLA Modules:
  0.0 57.0 jit_solution(3135121887194708029)
XLA Ops:
  0.0 56.0 %solve.1 = f32[1024,256]{1,0:T(8,128)S(1)} custom-call(f32[1024,256]{1,0:T(8,128)} %rs_hbm.1, f32[4,4,1024]{2,1,0:T(4,128)} %fac.1, f32[4,4,256]{2,1,0:T(4,128)} %inv.1), custom_call_target="tpu_custom_call" | custom-call | flops 2147483648 | bytes 8388608 | tf_op jit(solution)/shard_map/solve/pallas_call | solution.py:526
  56.0 1.0 %copy.5 = f32[1024,256]{1,0:T(8,128)} copy(f32[1024,256]{1,0:T(8,128)S(1)} %solve.1) | data formatting | bytes 2097152

commit v4 on v3

--- a/solution.py
+++ b/solution.py
@@ -301,6 +301,19 @@
         spread(0, 0, h)
 
     def steps(j, carry):
+        for h in (0, 1):
+            for d in (0, 1):
+                small_arrival(2 * j, d, h).wait_recv()
+                if h == d:
+                    tree(2 * j, 2, d, h).start()
+                else:
+
+                    @pl.when(j < 3)
+                    def _(d=d, h=h):
+                        tree(2 * j, 2, d, h).start()
+
+                tree(2 * j, 1, d, h).start()
+                spread(2 * j, d, h)
         for c in range(len(CHUNKS)):
             for d in (0, 1):
                 arrival(2 * j, d, c).wait_recv()
@@ -316,24 +329,7 @@
                 hand_on(2 * j, d, c)
         for h in (0, 1):
             for d in (0, 1):
-                small_arrival(2 * j, d, h).wait_recv()
-                if h == d:
-                    tree(2 * j, 2, d, h).start()
-                else:
-
-                    @pl.when(j < 3)
-                    def _(d=d, h=h):
-                        tree(2 * j, 2, d, h).start()
-
-                tree(2 * j, 1, d, h).start()
-                spread(2 * j, d, h)
-        for h in (0, 1):
-            for d in (0, 1):
                 take_odd(2 * j - 1, d, h)
-
-        for c in range(len(CHUNKS)):
-            for d in (0, 1):
-                take_end(2 * j - 1, d, c)
 
         @pl.when(j == 1)
         def _():
@@ -349,8 +345,6 @@
                 for d in (0, 1):
                     take_y(2 * j - 3, d, h)
                     take_y(2 * j - 2, d, h)
-            peer_arrivals(2 * j - 3)
-            peer_arrivals(2 * j - 2)
 
         @pl.when(j == 2)
         def _():
@@ -367,40 +361,48 @@
                     take_over(1, d, h)
                     take_over(2, d, h)
 
+        for c in range(len(CHUNKS)):
+            for d in (0, 1):
+                take_end(2 * j - 1, d, c)
+
+        @pl.when(j > 1)
+        def _():
+            peer_arrivals(2 * j - 3)
+            peer_arrivals(2 * j - 2)
+
         return carry
 
     lax.fori_loop(1, 4, steps, 0)
+    for h in (0, 1):
+        take_odd(8, h, h)
+    for h in (0, 1):
+        for d in (0, 1):
+            take_odd(7, d, h)
+    for h in (0, 1):
+        for d in (0, 1):
+            take_y(5, d, h)
+            take_y(6, d, h)
     for d, c in LAST:
         take_end(8, d, c)
     for h in (0, 1):
-        take_odd(8, h, h)
-    for h in (0, 1):
-        for d in (0, 1):
-            take_odd(7, d, h)
-    for c in range(len(CHUNKS)):
-        for d in (0, 1):
-            take_end(7, d, c)
-    for h in (0, 1):
-        for d in (0, 1):
-            take_y(5, d, h)
-            take_y(6, d, h)
+        for d in (0, 1):
             take_over(3, d, h)
             take_over(4, d, h)
-    peer_arrivals(5)
-    peer_arrivals(6)
     for h in (0, 1):
         take_y(8, h, h)
         for d in (0, 1):
             take_y(7, d, h)
+    for c in range(len(CHUNKS)):
+        for d in (0, 1):
+            take_end(7, d, c)
+    for h in (0, 1):
+        for d in (0, 1):
             take_over(5, d, h)
             take_over(6, d, h)
     for h in (0, 1):
         take_over(8, h, h)
         for d in (0, 1):
             take_over(7, d, h)
-
-    sib_small = small.at[1 - q]
-    pltpu.make_async_copy(sib_small, sib_small, sib_r.at[0]).wait()
 
     @pl.when(row < OWNERS)
     def _():
@@ -411,6 +413,11 @@
     b_wait(after, 0)
     for part in (0, 1):
         b_wait(over, part)
+
+    work = [bvec[k].T for k in range(PANELS)]
+
+    sib_small = small.at[1 - q]
+    pltpu.make_async_copy(sib_small, sib_small, sib_r.at[0]).wait()
 
     def prepare(place, carry):
         quarter, slot = place // SLOTS, place % SLOTS
@@ -426,22 +433,24 @@
     lax.fori_loop(9, 12, prepare, 0)
     load_rs.wait()
 
-    work = [bvec[k] for k in range(PANELS)]
     for k in range(PANELS):
         place = inverse_place(k)
-        answer = dot3((ahi[place], alo[place]), split(work[k]), ((1,), (0,)))
+        answer = dot3(split(work[k]), (ahi[place], alo[place]), ((1,), (1,)))
         x = split(answer)
         for m in range(k + 1, PANELS):
             place = block_place(k, m)
-            work[m] = work[m] - dot3((ahi[place], alo[place]), x, ((0,), (0,)))
+            work[m] = work[m] - dot3(x, (ahi[place], alo[place]), ((1,), (0,)))
 
         @pl.when(row == k)
         def _(answer=answer):
-            out[pl.ds(0, NB), :] = answer
-
-        xhi[k] = x[0].reshape(2, HALF, NB)
-        xlo[k] = x[1].reshape(2, HALF, NB)
+            out[pl.ds(0, NB), :] = answer.T
+
+        for half in (0, 1):
+            xhi[k, half] = x[0][:, half * HALF : (half + 1) * HALF]
+            xlo[k, half] = x[1][:, half * HALF : (half + 1) * HALF]
         if k == 1:
+            peer_arrivals(5)
+            peer_arrivals(6)
             peer_arrivals(7)
     for d, part in ((0, ONE), (1, TWO)):
         origin = origin_of(8, d)
@@ -460,12 +469,12 @@
         for group in parts:
             f = jnp.concatenate([factor(half, k) for half, k in group], axis=0)
             x = tuple(
-                jnp.concatenate([ref[k, half] for half, k in group], axis=0) for ref in (xhi, xlo)
+                jnp.concatenate([ref[k, half] for half, k in group], axis=1) for ref in (xhi, xlo)
             )
-            term = dot3(split(f), x, ((0,), (0,)))
+            term = dot3(x, split(f), ((1,), (0,)))
             total = term if total is None else total + term
         rows = pl.ds(pl.multiple_of(block * NB, NB), NB)
-        out[rows, :] = out[rows, :] - total
+        out[rows, :] = out[rows, :] - total.T
 
     def all_blocks(parts):
         def blocks(block, carry):
@@ -533,8 +542,8 @@
             pltpu.VMEM((2, 2, NZ, PANELS, 4, rows), F32),
             pltpu.VMEM((2, 4, NZ, 2, SLOTS, 4, NB), F32),
             pltpu.VMEM((OWNERS, NB, columns), F32),
-            pltpu.VMEM((PANELS, 2, HALF, columns), BF16),
-            pltpu.VMEM((PANELS, 2, HALF, columns), BF16),
+            pltpu.VMEM((PANELS, 2, columns, HALF), BF16),
+            pltpu.VMEM((PANELS, 2, columns, HALF), BF16),
             pltpu.VMEM((4 * SLOTS, NB, NB), BF16),
             pltpu.VMEM((4 * SLOTS, NB, NB), BF16),
             dma((8,)),

time: 57.1 us -> 55.6 us (0.974)
  Pallas kernels: 56 us -> 54.3 us
    pallas_call x1, Pallas kernels: 56 us -> 54.3 us  [per_device(): pl.pallas_call(kernel, name='solve', out_shape=pltpu.VMEM((rows, columns)...]
where the time goes in v4:
time: 55.6 us; the launch traced here: 55.3 us
  Pallas kernels  54.3 us (98%)
  local copies, waits for them, and re-layouts  0.97 us (2%)
    pallas_call x1, Pallas kernels, per_device(): pl.pallas_call(kernel, name='solve', out_shape=pltpu.VMEM((rows, columns)...  54.3 us

profile of v4, /device:TPU:1, one launch (start us, length us, event | category | flops | bytes accessed | tf_op | source)
XLA Modules:
  0.0 55.3 jit_solution(15544743592496991376)
XLA Ops:
  0.0 54.3 %solve.1 = f32[1024,256]{1,0:T(8,128)S(1)} custom-call(f32[1024,256]{1,0:T(8,128)} %rs_hbm.1, f32[4,4,1024]{2,1,0:T(4,128)} %fac.1, f32[4,4,256]{2,1,0:T(4,128)} %inv.1), custom_call_target="tpu_custom_call" | custom-call | flops 2147483648 | bytes 8388608 | tf_op jit(solution)/shard_map/solve/pallas_call | solution.py:535
  54.3 1.0 %copy.5 = f32[1024,256]{1,0:T(8,128)} copy(f32[1024,256]{1,0:T(8,128)S(1)} %solve.1) | data formatting | bytes 2097152

commit v5 on v4

--- a/solution.py
+++ b/solution.py
@@ -336,6 +336,7 @@
             from_peer(z, 0, 0, REST).wait_recv()
             peer_to_sibling(z, 0, 0, REST).start()
             forward_b(0)
+            forward_b(1)
             for h in (0, 1):
                 take_y(0, 0, h)
 
@@ -348,14 +349,13 @@
 
         @pl.when(j == 2)
         def _():
-            forward_b(1)
+            for part in (0, 1):
+                relay_b(part)
             for h in (0, 1):
                 take_over(0, 0, h)
 
         @pl.when(j == 3)
         def _():
-            for part in (0, 1):
-                relay_b(part)
             for h in (0, 1):
                 for d in (0, 1):
                     take_over(1, d, h)

time: 55.6 us -> 55.1 us (level)
  Pallas kernels: 54.3 us -> 53.5 us
    pallas_call x1, Pallas kernels: 54.3 us -> 53.5 us  [per_device(): pl.pallas_call(kernel, name='solve', out_shape=pltpu.VMEM((rows, columns)...]
where the time goes in v5:
time: 55.1 us; the launch traced here: 54.5 us
  Pallas kernels  53.5 us (97%)
  local copies, waits for them, and re-layouts  0.97 us (2%)
    pallas_call x1, Pallas kernels, per_device(): pl.pallas_call(kernel, name='solve', out_shape=pltpu.VMEM((rows, columns)...  53.5 us

profile of v5, /device:TPU:1, one launch (start us, length us, event | category | flops | bytes accessed | tf_op | source)
XLA Modules:
  0.0 54.5 jit_solution(8551388493552570611)
XLA Ops:
  0.0 53.5 %solve.1 = f32[1024,256]{1,0:T(8,128)S(1)} custom-call(f32[1024,256]{1,0:T(8,128)} %rs_hbm.1, f32[4,4,1024]{2,1,0:T(4,128)} %fac.1, f32[4,4,256]{2,1,0:T(4,128)} %inv.1), custom_call_target="tpu_custom_call" | custom-call | flops 2147483648 | bytes 8388608 | tf_op jit(solution)/shard_map/solve/pallas_call | solution.py:535
  53.5 1.0 %copy.5 = f32[1024,256]{1,0:T(8,128)} copy(f32[1024,256]{1,0:T(8,128)S(1)} %solve.1) | data formatting | bytes 2097152

commit v6 on v5

--- a/solution.py
+++ b/solution.py
@@ -300,6 +300,8 @@
             tree(0, 1, d, h).start()
         spread(0, 0, h)
 
+    forward_b(0)
+
     def steps(j, carry):
         for h in (0, 1):
             for d in (0, 1):
@@ -335,7 +337,6 @@
         def _():
             from_peer(z, 0, 0, REST).wait_recv()
             peer_to_sibling(z, 0, 0, REST).start()
-            forward_b(0)
             forward_b(1)
             for h in (0, 1):
                 take_y(0, 0, h)

time: 55.1 us -> 54.6 us (level)
  no operation moved by 1% of the time
where the time goes in v6:
time: 54.6 us; the launch traced here: 54.5 us
  Pallas kernels  53.5 us (98%)
  local copies, waits for them, and re-layouts  0.97 us (2%)
    pallas_call x1, Pallas kernels, per_device(): pl.pallas_call(kernel, name='solve', out_shape=pltpu.VMEM((rows, columns)...  53.5 us

profile of v6, /device:TPU:1, one launch (start us, length us, event | category | flops | bytes accessed | tf_op | source)
XLA Modules:
  0.0 54.5 jit_solution(8249674736556229504)
XLA Ops:
  0.0 53.5 %solve.1 = f32[1024,256]{1,0:T(8,128)S(1)} custom-call(f32[1024,256]{1,0:T(8,128)} %rs_hbm.1, f32[4,4,1024]{2,1,0:T(4,128)} %fac.1, f32[4,4,256]{2,1,0:T(4,128)} %inv.1), custom_call_target="tpu_custom_call" | custom-call | flops 2147483648 | bytes 8388608 | tf_op jit(solution)/shard_map/solve/pallas_call | solution.py:536
  53.5 1.0 %copy.5 = f32[1024,256]{1,0:T(8,128)} copy(f32[1024,256]{1,0:T(8,128)S(1)} %solve.1) | data formatting | bytes 2097152
